TPU v7x, 32 devices: a whole 2x2x4 slice. The times are simulated.
32 devices in a mesh: sections: 2 (over x), chan: 16 (over z, y, core).
Axes of the slice: x: 2, y: 2, z: 4, core: 2. Of those that a mesh axis runs over, the one named last changes fastest.
Arguments:
- raw_field: bfloat16 [65536, 1024], P('chan', 'sections'), parts along dimension 1, may hold values from -12 to 12
- bin_list: int32 [128], replicated, may hold values from 1 to 1023, as said below
Outputs:
- cross_spectra: bfloat16 [1024, 512, 256], P(('sections', 'chan')), parts along dimension 0
There are 2 independent parts, one for each index of `sections`. A program takes and returns all parts, laid end to end along the dimension named above; an argument that names none is the same for every part. Nothing has to cross between parts.
Inputs may be any that keep to these rules, and one draw needn't show every extreme that they name: `bin_list`: 128 distinct bin numbers in increasing order.
All inputs are finite; a program needn't handle non-finite values.
Results may differ from a plain program's by a relative error of at most 0.023.
Values may be sent and summed in bfloat16 or wider, within the bound.
A program may use at most 128 MiB of HBM per device.

v0:
```python
import math

import jax
import jax.numpy as jnp
import numpy as np
from jax import lax
from jax.sharding import PartitionSpec as P


def shifted(x, axis, by):
    length = lax.axis_size(axis)
    pairs = [(i, i + by) for i in range(length) if 0 <= i + by < length]
    return lax.ppermute(x, axis, pairs)


def passed_along(x, axis, by):
    length = lax.axis_size(axis)
    return lax.ppermute(x, axis, [(i, (i + by) % length) for i in range(length)])


def lowpass_taps():
    shaped = []
    for offset in range(32):
        where = (offset - 15.5) / 4.0
        sinc_value = math.sin(math.pi * where) / (math.pi * where)
        hamming_value = 0.54 - 0.46 * math.cos(2.0 * math.pi * offset / 31.0)
        shaped.append(sinc_value * hamming_value)
    total = sum(shaped)
    return np.array([value / total for value in shaped], np.float32)


def phase_taps():
    filter_taps = lowpass_taps()
    table_rows = np.zeros((9, 4), np.float32)
    for block in range(9):
        for phase in range(4):
            offset = 32 - 4 * block - phase
            if 0 <= offset <= 31:
                table_rows[block, phase] = filter_taps[offset]
    return table_rows


def hann_window(length):
    positions = jnp.arange(length, dtype=jnp.int32).astype(jnp.float32)
    return jnp.sin(math.pi * positions / length) ** 2


def window_power(length):
    return jnp.sum(hann_window(length) ** 2)


def fourier_table(bin_list, length):
    positions = jnp.arange(length, dtype=jnp.int32)
    phases = (positions[:, None] * bin_list[None, :] % length).astype(jnp.float32) * (
        2.0 * math.pi / length
    )
    window = hann_window(length)[:, None]
    cosines = window * jnp.cos(phases)
    sines = -window * jnp.sin(phases)
    half_len = length // 2
    leading = jnp.concatenate([cosines[:half_len], sines[:half_len]], 1)
    trailing = jnp.concatenate([cosines[half_len:], sines[half_len:]], 1)
    return jnp.concatenate([leading, trailing], 1).astype(jnp.bfloat16)


def decimate(padded, out_rows):
    channels = padded.shape[1]
    full_pad = jnp.concatenate([jnp.zeros((1, channels), padded.dtype), padded], 0)
    grouped = full_pad.reshape(out_rows + 8, 4, channels)
    taps_table = jnp.asarray(phase_taps())
    summed = jnp.zeros((out_rows, channels), jnp.float32)
    for block in range(9):
        window_rows = grouped[block : block + out_rows]
        summed = summed + jnp.einsum(
            "nrc,r->nc", window_rows, taps_table[block], preferred_element_type=jnp.float32
        )
    return summed.astype(jnp.bfloat16)


def cross_parts(left_re, left_im, right_re, right_im):

    def inner(first_op, second_op):
        return jnp.einsum("sif,sjf->ijf", first_op, second_op, preferred_element_type=jnp.float32)

    real_part = inner(left_re, right_re) + inner(left_im, right_im)
    imag_part = inner(left_im, right_re) - inner(left_re, right_im)
    return (real_part, imag_part)


def cross_block(left_tile, right_tile, bin_count):
    real_part, imag_part = cross_parts(
        left_tile[..., :bin_count],
        left_tile[..., bin_count:],
        right_tile[..., :bin_count],
        right_tile[..., bin_count:],
    )
    return jnp.concatenate([real_part, imag_part], -1)


def per_device(raw_field, bin_list):
    row_count, channels = raw_field.shape
    half_len = row_count // 4
    bin_count = bin_list.shape[0]
    dev_count = lax.axis_size("chan")
    dev_index = lax.axis_index("chan")
    rim_rows = shifted(raw_field[row_count - 31 :], "chan", 1)
    padded = jnp.concatenate([rim_rows, raw_field], 0)
    decimated = decimate(padded, half_len)
    fourier = fourier_table(bin_list, 2 * half_len)
    partial_value = jnp.einsum("nc,nf->cf", decimated, fourier, preferred_element_type=jnp.float32)
    next_part = shifted(partial_value[:, 2 * bin_count :], "chan", -1)
    has_segment = (dev_index < dev_count - 1).astype(jnp.float32)
    spectrum = ((partial_value[:, : 2 * bin_count] + next_part) * has_segment).astype(jnp.bfloat16)
    normalizer = 1.0 / ((dev_count - 1) * window_power(2 * half_len))
    block_cols = channels // dev_count
    zero_index = jnp.zeros((), jnp.int32)
    result = jnp.zeros((block_cols, channels, 2 * bin_count), jnp.bfloat16)
    tile_set = lax.all_to_all(spectrum[None], "chan", split_axis=1, concat_axis=0, tiled=True)

    def place_block(output, holding, source):
        product = (cross_block(tile_set, holding, bin_count) * normalizer).astype(jnp.bfloat16)
        return lax.dynamic_update_slice(
            output, product, (zero_index, source * block_cols, zero_index)
        )

    result = place_block(result, tile_set, dev_index)

    def advance_full(turn_number, state):
        holding, output = state
        holding = passed_along(holding, "chan", 1)
        return (holding, place_block(output, holding, (dev_index - turn_number) % dev_count))

    result = lax.fori_loop(1, dev_count, advance_full, (tile_set, result))[1]
    return result


def solution(mesh):
    placed = (P("chan", "sections"), P())
    return jax.shard_map(
        per_device,
        mesh=mesh,
        in_specs=placed,
        out_specs=P(("sections", "chan"), None, None),
        check_vma=False,
    )
```

profile of v0, /device:TPU:0, one launch (start us, length us, event | category | flops | bytes accessed | tf_op | source)
XLA Modules:
  0.0 635.2 jit_solution(5541938862843998427)
XLA Ops:
  3.3 6.9 %slice.184 = bf16[1024,4,512]{2,1,0:T(4,128)(2,1)} reshape(bf16[4096,512]{1,0:T(8,128)(2,1)} %param.5) | data formatting | bytes 8388608 | tf_op jit(solution)/shard_map/slice | solution.py:73
  20.3 9.9 %fusion.9 = (bf16[4096,512]{1,0:T(8,128)(2,1)}, bf16[4096,512]{1,0:T(8,128)(2,1)}, bf16[4096,512]{1,0:T(8,128)(2,1)}, bf16[4096,512]{1,0:T(8,128)(2,1)}, bf16[40...) fusion(bf16[31,512]{1,0:T(8,128)(2,1)S(1)} %collective-permute-done.1, ...), kind=kLoop, calls=%fused_computation.18 | loop fusion | flops 58720256 | bytes 33586176 | tf_op jit(solution)/shard_map/concatenate | solution.py:68
  30.2 6.9 %slice.164 = bf16[1024,4,512]{2,1,0:T(4,128)(2,1)} reshape(bf16[4096,512]{1,0:T(8,128)(2,1)} %get-tuple-element.193) | data formatting | bytes 8388608 | tf_op jit(solution)/shard_map/slice | solution.py:73
  37.1 6.9 %slice.167 = bf16[1024,4,512]{2,1,0:T(4,128)(2,1)} reshape(bf16[4096,512]{1,0:T(8,128)(2,1)} %get-tuple-element.194) | data formatting | bytes 8388608 | tf_op jit(solution)/shard_map/slice | solution.py:73
  44.0 6.9 %slice.170 = bf16[1024,4,512]{2,1,0:T(4,128)(2,1)} reshape(bf16[4096,512]{1,0:T(8,128)(2,1)} %get-tuple-element.195) | data formatting | bytes 8388608 | tf_op jit(solution)/shard_map/slice | solution.py:73
  51.0 6.9 %slice.173 = bf16[1024,4,512]{2,1,0:T(4,128)(2,1)} reshape(bf16[4096,512]{1,0:T(8,128)(2,1)} %get-tuple-element.196) | data formatting | bytes 8388608 | tf_op jit(solution)/shard_map/slice | solution.py:73
  57.9 6.9 %slice.176 = bf16[1024,4,512]{2,1,0:T(4,128)(2,1)} reshape(bf16[4096,512]{1,0:T(8,128)(2,1)} %get-tuple-element.197) | data formatting | bytes 8388608 | tf_op jit(solution)/shard_map/slice | solution.py:73
  64.8 6.9 %slice.179 = bf16[1024,4,512]{2,1,0:T(4,128)(2,1)} reshape(bf16[4096,512]{1,0:T(8,128)(2,1)} %get-tuple-element.199) | data formatting | bytes 8388608 | tf_op jit(solution)/shard_map/slice | solution.py:73
  71.7 6.9 %slice.182 = bf16[1024,4,512]{2,1,0:T(4,128)(2,1)} reshape(bf16[4096,512]{1,0:T(8,128)(2,1)} %get-tuple-element.198) | data formatting | bytes 8388608 | tf_op jit(solution)/shard_map/slice | solution.py:73
  78.7 19.8 %concatenate.29 = bf16[4128,512]{1,0:T(8,128)(2,1)} concatenate(bf16[1,512]{1,0:T(2,128)(2,1)S(1)} %broadcast_in_dim.12, bf16[31,512]{1,0:T(8,128)(2,1)S(1)} %collective-permute-done.1, bf16[4096,512]{1,0:T(8,128)(2,1)} %param.5), dimensions={0} | concatenate | bytes 8454144 | tf_op jit(solution)/shard_map/concatenate | solution.py:68
  102.9 7.1 %slice.161 = bf16[1024,4,512]{2,1,0:T(4,128)(2,1)} reshape(bf16[4096,512]{1,0:T(8,128)(2,1)} %slice.196) | data formatting | bytes 8388608 | tf_op jit(solution)/shard_map/slice | solution.py:73
  133.3 5.8 fusion.53
  139.2 5.8 fusion.46
  145.0 5.2 fusion.18
  160.2 12.9 %all-to-all-start = ((bf16[16,2,4096]{2,1,0:T(2,128)(2,1)}), bf16[16,2,4096]{2,1,0:T(2,128)(2,1)S(1)}, u32[]{:S(2)}, u32[]{:S(2)}) async-start(bf16[16,2,4096]{2,1,0:T(2,128)(2,1)} %reshape.43), calls=%async_computation | async-start | bytes 524288 | tf_op jit(solution)/shard_map/all_to_all | solution.py:118
  174.3 8.8 %all-to-all-done = bf16[16,2,4096]{2,1,0:T(2,128)(2,1)S(1)} async-done(((bf16[16,2,4096]{2,1,0:T(2,128)(2,1)}), bf16[16,2,4096]{2,1,0:T(2,128)(2,1)S(1)}, u32[]{:S(2)}, u32[]{:S(2)}) %all-to-all-start) | async-done | bytes 262176 | tf_op jit(solution)/shard_map/all_to_all | solution.py:118
  199.8 435.0 %while.17 = (s32[]{:T(128)}, bf16[16,32,256]{2,1,0:T(8,128)(2,1)S(1)}, bf16[32,512,256]{2,1,0:T(8,128)(2,1)}, bf16[16,32,256]{1,0,2:T(8,128)(2,1)S(1)}, f32[]{:T...) while((s32[]{:T(128)}, ...), condition=%wide.region_2.3_spmd, body=%wide.region_1.2_spmd.sunk | while | flops 17825808 | bytes 14549860 | solution.py:133
  199.8 8.5 %collective-permute-done = bf16[16,32,256]{2,1,0:T(8,128)(2,1)S(1)} collective-permute-done((bf16[16,32,256]{2,1,0:T(8,128)(2,1)S(1)}, bf16[16,32,256]{2,1,0:T(8,128)(2,1)S(1)}, u32[]{:S(2)}, u32[]{:S(2)}) %collective-permute-start) | collective-permute-done | bytes 262176 | tf_op jit(solution)/shard_map/while/body/eval_jaxpr/ppermute | solution.py:18
  228.8 8.5 %collective-permute-done = bf16[16,32,256]{2,1,0:T(8,128)(2,1)S(1)} collective-permute-done((bf16[16,32,256]{2,1,0:T(8,128)(2,1)S(1)}, bf16[16,32,256]{2,1,0:T(8,128)(2,1)S(1)}, u32[]{:S(2)}, u32[]{:S(2)}) %collective-permute-start) | collective-permute-done | bytes 262176 | tf_op jit(solution)/shard_map/while/body/eval_jaxpr/ppermute | solution.py:18
  257.8 8.5 %collective-permute-done = bf16[16,32,256]{2,1,0:T(8,128)(2,1)S(1)} collective-permute-done((bf16[16,32,256]{2,1,0:T(8,128)(2,1)S(1)}, bf16[16,32,256]{2,1,0:T(8,128)(2,1)S(1)}, u32[]{:S(2)}, u32[]{:S(2)}) %collective-permute-start) | collective-permute-done | bytes 262176 | tf_op jit(solution)/shard_map/while/body/eval_jaxpr/ppermute | solution.py:18
  286.8 8.5 %collective-permute-done = bf16[16,32,256]{2,1,0:T(8,128)(2,1)S(1)} collective-permute-done((bf16[16,32,256]{2,1,0:T(8,128)(2,1)S(1)}, bf16[16,32,256]{2,1,0:T(8,128)(2,1)S(1)}, u32[]{:S(2)}, u32[]{:S(2)}) %collective-permute-start) | collective-permute-done | bytes 262176 | tf_op jit(solution)/shard_map/while/body/eval_jaxpr/ppermute | solution.py:18
  315.8 8.5 %collective-permute-done = bf16[16,32,256]{2,1,0:T(8,128)(2,1)S(1)} collective-permute-done((bf16[16,32,256]{2,1,0:T(8,128)(2,1)S(1)}, bf16[16,32,256]{2,1,0:T(8,128)(2,1)S(1)}, u32[]{:S(2)}, u32[]{:S(2)}) %collective-permute-start) | collective-permute-done | bytes 262176 | tf_op jit(solution)/shard_map/while/body/eval_jaxpr/ppermute | solution.py:18
  344.8 8.5 %collective-permute-done = bf16[16,32,256]{2,1,0:T(8,128)(2,1)S(1)} collective-permute-done((bf16[16,32,256]{2,1,0:T(8,128)(2,1)S(1)}, bf16[16,32,256]{2,1,0:T(8,128)(2,1)S(1)}, u32[]{:S(2)}, u32[]{:S(2)}) %collective-permute-start) | collective-permute-done | bytes 262176 | tf_op jit(solution)/shard_map/while/body/eval_jaxpr/ppermute | solution.py:18
  373.9 8.5 %collective-permute-done = bf16[16,32,256]{2,1,0:T(8,128)(2,1)S(1)} collective-permute-done((bf16[16,32,256]{2,1,0:T(8,128)(2,1)S(1)}, bf16[16,32,256]{2,1,0:T(8,128)(2,1)S(1)}, u32[]{:S(2)}, u32[]{:S(2)}) %collective-permute-start) | collective-permute-done | bytes 262176 | tf_op jit(solution)/shard_map/while/body/eval_jaxpr/ppermute | solution.py:18
  402.9 8.5 %collective-permute-done = bf16[16,32,256]{2,1,0:T(8,128)(2,1)S(1)} collective-permute-done((bf16[16,32,256]{2,1,0:T(8,128)(2,1)S(1)}, bf16[16,32,256]{2,1,0:T(8,128)(2,1)S(1)}, u32[]{:S(2)}, u32[]{:S(2)}) %collective-permute-start) | collective-permute-done | bytes 262176 | tf_op jit(solution)/shard_map/while/body/eval_jaxpr/ppermute | solution.py:18
  431.9 8.5 %collective-permute-done = bf16[16,32,256]{2,1,0:T(8,128)(2,1)S(1)} collective-permute-done((bf16[16,32,256]{2,1,0:T(8,128)(2,1)S(1)}, bf16[16,32,256]{2,1,0:T(8,128)(2,1)S(1)}, u32[]{:S(2)}, u32[]{:S(2)}) %collective-permute-start) | collective-permute-done | bytes 262176 | tf_op jit(solution)/shard_map/while/body/eval_jaxpr/ppermute | solution.py:18
  460.9 8.5 %collective-permute-done = bf16[16,32,256]{2,1,0:T(8,128)(2,1)S(1)} collective-permute-done((bf16[16,32,256]{2,1,0:T(8,128)(2,1)S(1)}, bf16[16,32,256]{2,1,0:T(8,128)(2,1)S(1)}, u32[]{:S(2)}, u32[]{:S(2)}) %collective-permute-start) | collective-permute-done | bytes 262176 | tf_op jit(solution)/shard_map/while/body/eval_jaxpr/ppermute | solution.py:18
  489.9 8.5 %collective-permute-done = bf16[16,32,256]{2,1,0:T(8,128)(2,1)S(1)} collective-permute-done((bf16[16,32,256]{2,1,0:T(8,128)(2,1)S(1)}, bf16[16,32,256]{2,1,0:T(8,128)(2,1)S(1)}, u32[]{:S(2)}, u32[]{:S(2)}) %collective-permute-start) | collective-permute-done | bytes 262176 | tf_op jit(solution)/shard_map/while/body/eval_jaxpr/ppermute | solution.py:18
  518.9 8.5 %collective-permute-done = bf16[16,32,256]{2,1,0:T(8,128)(2,1)S(1)} collective-permute-done((bf16[16,32,256]{2,1,0:T(8,128)(2,1)S(1)}, bf16[16,32,256]{2,1,0:T(8,128)(2,1)S(1)}, u32[]{:S(2)}, u32[]{:S(2)}) %collective-permute-start) | collective-permute-done | bytes 262176 | tf_op jit(solution)/shard_map/while/body/eval_jaxpr/ppermute | solution.py:18
  547.9 8.5 %collective-permute-done = bf16[16,32,256]{2,1,0:T(8,128)(2,1)S(1)} collective-permute-done((bf16[16,32,256]{2,1,0:T(8,128)(2,1)S(1)}, bf16[16,32,256]{2,1,0:T(8,128)(2,1)S(1)}, u32[]{:S(2)}, u32[]{:S(2)}) %collective-permute-start) | collective-permute-done | bytes 262176 | tf_op jit(solution)/shard_map/while/body/eval_jaxpr/ppermute | solution.py:18
  576.9 8.5 %collective-permute-done = bf16[16,32,256]{2,1,0:T(8,128)(2,1)S(1)} collective-permute-done((bf16[16,32,256]{2,1,0:T(8,128)(2,1)S(1)}, bf16[16,32,256]{2,1,0:T(8,128)(2,1)S(1)}, u32[]{:S(2)}, u32[]{:S(2)}) %collective-permute-start) | collective-permute-done | bytes 262176 | tf_op jit(solution)/shard_map/while/body/eval_jaxpr/ppermute | solution.py:18
  605.9 8.5 %collective-permute-done = bf16[16,32,256]{2,1,0:T(8,128)(2,1)S(1)} collective-permute-done((bf16[16,32,256]{2,1,0:T(8,128)(2,1)S(1)}, bf16[16,32,256]{2,1,0:T(8,128)(2,1)S(1)}, u32[]{:S(2)}, u32[]{:S(2)}) %collective-permute-start) | collective-permute-done | bytes 262176 | tf_op jit(solution)/shard_map/while/body/eval_jaxpr/ppermute | solution.py:18
  (280 shorter events, 375.2 us)
Async XLA Ops:
  0.8 19.5 %collective-permute-start.1 = (bf16[31,512]{1,0:T(8,128)(2,1)S(1)}, bf16[31,512]{1,0:T(8,128)(2,1)S(1)}, u32[]{:S(2)}, u32[]{:S(2)}) collective-permute-start(bf16[31,512]{1,0:T(8,128)(2,1)S(1)} %slice.159), channel_id=1, source_target_pairs={{0,1},{1,2},{2,3},{3,4},{4,5},{5,6},{6,7},{7,8},{8,9},{9,10},{10,1... | collective-permute-start | bytes 95240 | tf_op jit(solution)/shard_map/ppermute | solution.py:13
  3.3 6.9 %copy-start.17 = (bf16[4,1,1]{0,1,2:T(2,128)(2,1)S(1)}, bf16[4,1,1]{0,1,2:T(2,128)(2,1)}, u32[]{:S(2)}) copy-start(bf16[4,1,1]{0,1,2:T(2,128)(2,1)} %constant.197) | copy-start | bytes 28
  10.2 4.7 copy-start.8
  10.2 10.1 %copy-start.1 = (bf16[4096,512]{1,0:T(8,128)(2,1)S(1)}, bf16[4096,512]{1,0:T(8,128)(2,1)}, u32[]{:S(2)}) copy-start(bf16[4096,512]{1,0:T(8,128)(2,1)} %param.5) | copy-start | bytes 12582916
  102.9 7.1 %copy-start.16 = (bf16[4,1,1]{0,1,2:T(2,128)(2,1)S(1)}, bf16[4,1,1]{0,1,2:T(2,128)(2,1)}, u32[]{:S(2)}) copy-start(bf16[4,1,1]{0,1,2:T(2,128)(2,1)} %constant.204) | copy-start | bytes 28
  110.0 4.7 copy-start.4
  110.0 4.7 copy-start.15
  117.0 4.7 copy-start.3
  117.0 4.7 copy-start.13
  121.7 2.3 copy-start.12
  124.0 4.5 copy-start.11
  128.6 4.8 copy-start.10
  133.3 5.8 copy-start.9
  150.2 5.9 collective-permute-start.2
  160.2 22.9 %all-to-all-start = ((bf16[16,2,4096]{2,1,0:T(2,128)(2,1)}), bf16[16,2,4096]{2,1,0:T(2,128)(2,1)S(1)}, u32[]{:S(2)}, u32[]{:S(2)}) async-start(bf16[16,2,4096]{2,1,0:T(2,128)(2,1)} %reshape.43), calls=%async_computation | async-start | bytes 524288 | tf_op jit(solution)/shard_map/all_to_all | solution.py:118
  195.3 4.5 copy-start.7
  196.4 3.4 copy-start.2
  199.8 8.5 %collective-permute-start = (bf16[16,32,256]{2,1,0:T(8,128)(2,1)S(1)}, bf16[16,32,256]{2,1,0:T(8,128)(2,1)S(1)}, u32[]{:S(2)}, u32[]{:S(2)}) collective-permute-start(bf16[16,32,256]{2,1,0:T(8,128)(2,1)S(1)} %get-tuple-element.262), channel_id=1, source_target_pairs={{0,1},{1,2},{2,3},{3,4},{4,5},{5,6},{6,7},{7,8},{8,9},{9,10},{10,1... | collective-permute-start | bytes 786440 | tf_op jit(solution)/shard_map/while/body/eval_jaxpr/ppermute | solution.py:18
  228.8 8.5 %collective-permute-start = (bf16[16,32,256]{2,1,0:T(8,128)(2,1)S(1)}, bf16[16,32,256]{2,1,0:T(8,128)(2,1)S(1)}, u32[]{:S(2)}, u32[]{:S(2)}) collective-permute-start(bf16[16,32,256]{2,1,0:T(8,128)(2,1)S(1)} %get-tuple-element.262), channel_id=1, source_target_pairs={{0,1},{1,2},{2,3},{3,4},{4,5},{5,6},{6,7},{7,8},{8,9},{9,10},{10,1... | collective-permute-start | bytes 786440 | tf_op jit(solution)/shard_map/while/body/eval_jaxpr/ppermute | solution.py:18
  257.8 8.5 %collective-permute-start = (bf16[16,32,256]{2,1,0:T(8,128)(2,1)S(1)}, bf16[16,32,256]{2,1,0:T(8,128)(2,1)S(1)}, u32[]{:S(2)}, u32[]{:S(2)}) collective-permute-start(bf16[16,32,256]{2,1,0:T(8,128)(2,1)S(1)} %get-tuple-element.262), channel_id=1, source_target_pairs={{0,1},{1,2},{2,3},{3,4},{4,5},{5,6},{6,7},{7,8},{8,9},{9,10},{10,1... | collective-permute-start | bytes 786440 | tf_op jit(solution)/shard_map/while/body/eval_jaxpr/ppermute | solution.py:18
  286.8 8.5 %collective-permute-start = (bf16[16,32,256]{2,1,0:T(8,128)(2,1)S(1)}, bf16[16,32,256]{2,1,0:T(8,128)(2,1)S(1)}, u32[]{:S(2)}, u32[]{:S(2)}) collective-permute-start(bf16[16,32,256]{2,1,0:T(8,128)(2,1)S(1)} %get-tuple-element.262), channel_id=1, source_target_pairs={{0,1},{1,2},{2,3},{3,4},{4,5},{5,6},{6,7},{7,8},{8,9},{9,10},{10,1... | collective-permute-start | bytes 786440 | tf_op jit(solution)/shard_map/while/body/eval_jaxpr/ppermute | solution.py:18
  315.8 8.5 %collective-permute-start = (bf16[16,32,256]{2,1,0:T(8,128)(2,1)S(1)}, bf16[16,32,256]{2,1,0:T(8,128)(2,1)S(1)}, u32[]{:S(2)}, u32[]{:S(2)}) collective-permute-start(bf16[16,32,256]{2,1,0:T(8,128)(2,1)S(1)} %get-tuple-element.262), channel_id=1, source_target_pairs={{0,1},{1,2},{2,3},{3,4},{4,5},{5,6},{6,7},{7,8},{8,9},{9,10},{10,1... | collective-permute-start | bytes 786440 | tf_op jit(solution)/shard_map/while/body/eval_jaxpr/ppermute | solution.py:18
  344.8 8.5 %collective-permute-start = (bf16[16,32,256]{2,1,0:T(8,128)(2,1)S(1)}, bf16[16,32,256]{2,1,0:T(8,128)(2,1)S(1)}, u32[]{:S(2)}, u32[]{:S(2)}) collective-permute-start(bf16[16,32,256]{2,1,0:T(8,128)(2,1)S(1)} %get-tuple-element.262), channel_id=1, source_target_pairs={{0,1},{1,2},{2,3},{3,4},{4,5},{5,6},{6,7},{7,8},{8,9},{9,10},{10,1... | collective-permute-start | bytes 786440 | tf_op jit(solution)/shard_map/while/body/eval_jaxpr/ppermute | solution.py:18
  373.8 8.5 %collective-permute-start = (bf16[16,32,256]{2,1,0:T(8,128)(2,1)S(1)}, bf16[16,32,256]{2,1,0:T(8,128)(2,1)S(1)}, u32[]{:S(2)}, u32[]{:S(2)}) collective-permute-start(bf16[16,32,256]{2,1,0:T(8,128)(2,1)S(1)} %get-tuple-element.262), channel_id=1, source_target_pairs={{0,1},{1,2},{2,3},{3,4},{4,5},{5,6},{6,7},{7,8},{8,9},{9,10},{10,1... | collective-permute-start | bytes 786440 | tf_op jit(solution)/shard_map/while/body/eval_jaxpr/ppermute | solution.py:18
  402.8 8.5 %collective-permute-start = (bf16[16,32,256]{2,1,0:T(8,128)(2,1)S(1)}, bf16[16,32,256]{2,1,0:T(8,128)(2,1)S(1)}, u32[]{:S(2)}, u32[]{:S(2)}) collective-permute-start(bf16[16,32,256]{2,1,0:T(8,128)(2,1)S(1)} %get-tuple-element.262), channel_id=1, source_target_pairs={{0,1},{1,2},{2,3},{3,4},{4,5},{5,6},{6,7},{7,8},{8,9},{9,10},{10,1... | collective-permute-start | bytes 786440 | tf_op jit(solution)/shard_map/while/body/eval_jaxpr/ppermute | solution.py:18
  431.8 8.5 %collective-permute-start = (bf16[16,32,256]{2,1,0:T(8,128)(2,1)S(1)}, bf16[16,32,256]{2,1,0:T(8,128)(2,1)S(1)}, u32[]{:S(2)}, u32[]{:S(2)}) collective-permute-start(bf16[16,32,256]{2,1,0:T(8,128)(2,1)S(1)} %get-tuple-element.262), channel_id=1, source_target_pairs={{0,1},{1,2},{2,3},{3,4},{4,5},{5,6},{6,7},{7,8},{8,9},{9,10},{10,1... | collective-permute-start | bytes 786440 | tf_op jit(solution)/shard_map/while/body/eval_jaxpr/ppermute | solution.py:18
  460.8 8.5 %collective-permute-start = (bf16[16,32,256]{2,1,0:T(8,128)(2,1)S(1)}, bf16[16,32,256]{2,1,0:T(8,128)(2,1)S(1)}, u32[]{:S(2)}, u32[]{:S(2)}) collective-permute-start(bf16[16,32,256]{2,1,0:T(8,128)(2,1)S(1)} %get-tuple-element.262), channel_id=1, source_target_pairs={{0,1},{1,2},{2,3},{3,4},{4,5},{5,6},{6,7},{7,8},{8,9},{9,10},{10,1... | collective-permute-start | bytes 786440 | tf_op jit(solution)/shard_map/while/body/eval_jaxpr/ppermute | solution.py:18
  489.8 8.5 %collective-permute-start = (bf16[16,32,256]{2,1,0:T(8,128)(2,1)S(1)}, bf16[16,32,256]{2,1,0:T(8,128)(2,1)S(1)}, u32[]{:S(2)}, u32[]{:S(2)}) collective-permute-start(bf16[16,32,256]{2,1,0:T(8,128)(2,1)S(1)} %get-tuple-element.262), channel_id=1, source_target_pairs={{0,1},{1,2},{2,3},{3,4},{4,5},{5,6},{6,7},{7,8},{8,9},{9,10},{10,1... | collective-permute-start | bytes 786440 | tf_op jit(solution)/shard_map/while/body/eval_jaxpr/ppermute | solution.py:18
  518.8 8.5 %collective-permute-start = (bf16[16,32,256]{2,1,0:T(8,128)(2,1)S(1)}, bf16[16,32,256]{2,1,0:T(8,128)(2,1)S(1)}, u32[]{:S(2)}, u32[]{:S(2)}) collective-permute-start(bf16[16,32,256]{2,1,0:T(8,128)(2,1)S(1)} %get-tuple-element.262), channel_id=1, source_target_pairs={{0,1},{1,2},{2,3},{3,4},{4,5},{5,6},{6,7},{7,8},{8,9},{9,10},{10,1... | collective-permute-start | bytes 786440 | tf_op jit(solution)/shard_map/while/body/eval_jaxpr/ppermute | solution.py:18
  547.8 8.5 %collective-permute-start = (bf16[16,32,256]{2,1,0:T(8,128)(2,1)S(1)}, bf16[16,32,256]{2,1,0:T(8,128)(2,1)S(1)}, u32[]{:S(2)}, u32[]{:S(2)}) collective-permute-start(bf16[16,32,256]{2,1,0:T(8,128)(2,1)S(1)} %get-tuple-element.262), channel_id=1, source_target_pairs={{0,1},{1,2},{2,3},{3,4},{4,5},{5,6},{6,7},{7,8},{8,9},{9,10},{10,1... | collective-permute-start | bytes 786440 | tf_op jit(solution)/shard_map/while/body/eval_jaxpr/ppermute | solution.py:18
  576.8 8.5 %collective-permute-start = (bf16[16,32,256]{2,1,0:T(8,128)(2,1)S(1)}, bf16[16,32,256]{2,1,0:T(8,128)(2,1)S(1)}, u32[]{:S(2)}, u32[]{:S(2)}) collective-permute-start(bf16[16,32,256]{2,1,0:T(8,128)(2,1)S(1)} %get-tuple-element.262), channel_id=1, source_target_pairs={{0,1},{1,2},{2,3},{3,4},{4,5},{5,6},{6,7},{7,8},{8,9},{9,10},{10,1... | collective-permute-start | bytes 786440 | tf_op jit(solution)/shard_map/while/body/eval_jaxpr/ppermute | solution.py:18
  605.8 8.5 %collective-permute-start = (bf16[16,32,256]{2,1,0:T(8,128)(2,1)S(1)}, bf16[16,32,256]{2,1,0:T(8,128)(2,1)S(1)}, u32[]{:S(2)}, u32[]{:S(2)}) collective-permute-start(bf16[16,32,256]{2,1,0:T(8,128)(2,1)S(1)} %get-tuple-element.262), channel_id=1, source_target_pairs={{0,1},{1,2},{2,3},{3,4},{4,5},{5,6},{6,7},{7,8},{8,9},{9,10},{10,1... | collective-permute-start | bytes 786440 | tf_op jit(solution)/shard_map/while/body/eval_jaxpr/ppermute | solution.py:18
  (18 other events, 16.2 us)
where the time goes:
time: 646 us; the launch traced here: 635 us
  local copies, waits for them, and re-layouts  231 us (36%)
  matrix products  198 us (31%)
  waiting for transfers between devices  140 us (22%)
  other arithmetic  46.5 us (7%)
  starting transfers between devices  17.3 us (3%)
    dot_general x64, matrix products, inner(): jnp.einsum('sif,sjf->ijf', first_op, second_op, preferred_element_type=jn...  153 us
    ppermute x15, waiting for transfers between devices, passed_along(): lax.ppermute(x, axis, [(i, (i + by) % length) for i in range(length)])  127 us
    slice x10, local copies, waits for them, and re-layouts, decimate(): window_rows = grouped[block:block + out_rows]  66.8 us
    add x16, local copies, waits for them, and re-layouts, cross_parts(): real_part = inner(left_re, right_re) + inner(left_im, right_im)  55.3 us
    sub x16, local copies, waits for them, and re-layouts, cross_parts(): imag_part = inner(left_im, right_re) - inner(left_re, right_im)  42.5 us
    dot_general x9, matrix products, decimate(): jnp.einsum('nrc,r->nc', window_rows, taps_table[block], preferred_element...  39.5 us
    while x75, local copies, waits for them, and re-layouts  36.2 us
    dynamic_update_slice x16, other arithmetic, place_block(): lax.dynamic_update_slice(output, product, (zero_index, source * block_col...  29 us
  transfers between devices with their start and end apart: 18, of which 17 were waited for; matrix products, arithmetic and copies ran while one was open for 3% of the time, Pallas kernels for 0%

commit v1 on v0

v1 whole, which is shorter than its diff:
```python
import functools
import math

import jax
import jax.numpy as jnp
import numpy as np
from jax import lax
from jax.experimental import pallas as pl
from jax.experimental.pallas import tpu as pltpu
from jax.sharding import PartitionSpec as P

TAPS = 32
GROUP = 8
MESH = pl.DeviceIdType.MESH


def lowpass_taps():
    shaped = []
    for offset in range(TAPS):
        where = (offset - 15.5) / 4.0
        sinc_value = math.sin(math.pi * where) / (math.pi * where)
        hamming_value = 0.54 - 0.46 * math.cos(2.0 * math.pi * offset / 31.0)
        shaped.append(sinc_value * hamming_value)
    total = sum(shaped)
    return np.array([value / total for value in shaped], np.float64)


def band_matrix(out_rows):
    h = lowpass_taps()
    n = np.arange(out_rows)[:, None]
    m = np.arange(TAPS + 4 * out_rows)[None, :] - TAPS
    k = 4 * n - m
    inside = (k >= 0) & (k < TAPS)
    return np.where(inside, h[np.clip(k, 0, TAPS - 1)], 0.0)


def write_table(bins_ref, table_ref, half_len):
    length = 2 * half_len
    bin_count = bins_ref.shape[1]
    step = 2.0 * math.pi / length
    rows = jnp.broadcast_to(bins_ref[...].astype(jnp.float32), (128, bin_count))
    bins = jnp.transpose(rows).astype(jnp.int32)
    lane = lax.broadcasted_iota(jnp.int32, (bin_count, 128), 1)
    fine = (lax.rem(bins * lane, length)).astype(jnp.float32) * step
    coarse = (lax.rem(bins * lane * 128, length)).astype(jnp.float32) * step
    fine_cos, fine_sin = jnp.cos(fine), jnp.sin(fine)
    coarse_cos, coarse_sin = jnp.cos(coarse), jnp.sin(coarse)
    sign = 1.0 - 2.0 * lax.rem(bins, 2).astype(jnp.float32)

    def interleave(cosines, sines):
        pieces = []
        for g in range(bin_count // GROUP):
            pieces.append(cosines[g * GROUP : (g + 1) * GROUP])
            pieces.append(sines[g * GROUP : (g + 1) * GROUP])
        return jnp.concatenate(pieces, 0).astype(jnp.bfloat16)

    row_lane = lax.broadcasted_iota(jnp.int32, (8, 128), 1)
    for a in range(half_len // 128):
        ca, sa = coarse_cos[:, a : a + 1], coarse_sin[:, a : a + 1]
        cosines = fine_cos * ca - fine_sin * sa
        sines = -(fine_sin * ca + fine_cos * sa)
        position = (row_lane + a * 128).astype(jnp.float32) * (math.pi / length)
        leading = (jnp.sin(position) ** 2)[:1]
        trailing = (jnp.cos(position) ** 2)[:1] * sign
        columns = slice(a * 128, (a + 1) * 128)
        table_ref[0, :, columns] = interleave(cosines * leading, sines * leading)
        table_ref[1, :, columns] = interleave(cosines * trailing, sines * trailing)


def gather_kernel(
    n, raw_ref, bins_ref, band_ref, all_ref,
    raw_buf, table_ref, dec_ref, lead_ref, trail_out, trail_in, own_ref,
    raw_sem, halo_send, halo_recv, trail_send, trail_recv,
    own_sem, own_sib_send, own_sib_recv, ring_send, ring_recv, sib_send, sib_recv,
):
    chunks, _, width = raw_buf.shape
    raw_rows = raw_ref.shape[0]
    half_len = raw_rows // 4
    block = band_ref.shape[0]
    span = band_ref.shape[1]
    ring = n // 2
    me = lax.axis_index("chan")
    core = lax.rem(me, 2)
    chip = me // 2
    spot = jnp.where(lax.rem(chip, 2) == 0, chip // 2, ring - 1 - chip // 2)

    def device_at(position, which):
        position = lax.rem(position + 2 * ring, ring)
        at = jnp.where(position < ring // 2, 2 * position, 2 * (ring - 1 - position) + 1)
        return 2 * at + which

    sibling = 2 * chip + 1 - core
    neighbours = (device_at(spot + 1, core), device_at(spot - 1, core))
    after, before = lax.rem(me + 1, n), lax.rem(me + n - 1, n)

    def raw_copy(c):
        return pltpu.make_async_copy(
            raw_ref.at[:, pl.ds(c * width, width)],
            raw_buf.at[c, pl.ds(TAPS, raw_rows)],
            raw_sem.at[c],
        )

    def remote(src, dst, send, recv, target):
        return pltpu.make_async_remote_copy(
            src_ref=src, dst_ref=dst, send_sem=send, recv_sem=recv,
            device_id={"chan": target}, device_id_type=MESH,
        )

    for c in range(chunks):
        raw_copy(c).start()
    barrier = pltpu.get_barrier_semaphore()
    partners = neighbours + (sibling, after, before)
    for partner in partners:
        pl.semaphore_signal(barrier, inc=1, device_id={"chan": partner}, device_id_type=MESH)
    pl.semaphore_wait(barrier, len(partners))

    def halo_copy(c):
        return remote(
            raw_ref.at[pl.ds(raw_rows - TAPS, TAPS), pl.ds(c * width, width)],
            raw_buf.at[c, pl.ds(0, TAPS)],
            halo_send.at[c], halo_recv.at[c], after,
        )

    def trail_copy(c):
        return remote(trail_out.at[c], trail_in.at[c], trail_send.at[c], trail_recv.at[c], before)

    @pl.when(me < n - 1)
    def _():
        for c in range(chunks):
            halo_copy(c).start()

    @pl.when(me == 0)
    def _():
        for c in range(chunks):
            raw_buf[c, pl.ds(0, TAPS)] = jnp.zeros((TAPS, width), raw_buf.dtype)

    @pl.when(me == n - 1)
    def _():
        trail_in[...] = jnp.zeros(trail_in.shape, trail_in.dtype)

    write_table(bins_ref, table_ref, half_len)

    for c in range(chunks):
        raw_copy(c).wait()

        @pl.when(me > 0)
        def _():
            halo_copy(c).wait_recv()

        for b in range(half_len // block):
            dec_ref[pl.ds(b * block, block)] = jnp.dot(
                band_ref[...],
                raw_buf[c, pl.ds(b * 4 * block, span)],
                preferred_element_type=jnp.float32,
            ).astype(jnp.bfloat16)
        trail_out[c] = jnp.dot(
            table_ref[1], dec_ref[...], preferred_element_type=jnp.float32
        ).astype(jnp.bfloat16)

        @pl.when(me > 0)
        def _():
            trail_copy(c).start()

        lead_ref[c] = jnp.dot(table_ref[0], dec_ref[...], preferred_element_type=jnp.float32)

    reach = [[ring // 2 - (c % 2), ring // 2 - 1 + (c % 2)] for c in range(chunks)]

    def owner(way, t, which):
        return device_at(spot - t if way == 0 else spot + t, which)

    def ring_copy(way, c, t, src, whose):
        return remote(
            src, all_ref.at[whose, c],
            ring_send.at[way, c, t], ring_recv.at[way, c, t], neighbours[way],
        )

    def sib_copy(way, c, t, whose):
        return remote(
            all_ref.at[whose, c], all_ref.at[whose, c],
            sib_send.at[way, c, t], sib_recv.at[way, c, t], sibling,
        )

    def own_sib_copy(c, whose):
        return remote(
            own_ref.at[c], all_ref.at[whose, c], own_sib_send.at[c], own_sib_recv.at[c], sibling
        )

    def own_copy(c):
        return pltpu.make_async_copy(own_ref.at[c], all_ref.at[me, c], own_sem.at[c])

    for c in range(chunks):

        @pl.when(me < n - 1)
        def _():
            trail_copy(c).wait_recv()

        total = lead_ref[c] + trail_in[c].astype(jnp.float32)
        own_ref[c] = jnp.where(me < n - 1, total, 0.0).astype(jnp.bfloat16)
        for way in range(2):
            if reach[c][way] > 0:
                ring_copy(way, c, 0, own_ref.at[c], me).start()
        own_sib_copy(c, me).start()
        own_copy(c).start()

    for t in range(1, ring // 2 + 1):
        for c in range(chunks):
            for way in range(2):
                if t <= reach[c][way]:
                    whose = owner(way, t, core)
                    ring_copy(way, c, t - 1, own_ref.at[c], whose).wait_recv()
                    if t < reach[c][way]:
                        ring_copy(way, c, t, all_ref.at[whose, c], whose).start()
                    sib_copy(way, c, t - 1, whose).start()

    for c in range(chunks):

        @pl.when(me < n - 1)
        def _():
            halo_copy(c).wait_send()

        @pl.when(me > 0)
        def _():
            trail_copy(c).wait_send()

        own_copy(c).wait()
        own_sib_copy(c, me).wait_send()
        own_sib_copy(c, sibling).wait_recv()
        for way in range(2):
            for t in range(1, reach[c][way] + 1):
                if t == 1:
                    ring_copy(way, c, 0, own_ref.at[c], me).wait_send()
                else:
                    whose = owner(way, t - 1, core)
                    ring_copy(way, c, t - 1, all_ref.at[whose, c], whose).wait_send()
                sib_copy(way, c, t - 1, owner(way, t, core)).wait_send()
                sib_copy(way, c, t - 1, owner(way, t, 1 - core)).wait_recv()


def cross_kernel(n, scale, all_ref, out_ref, left_ref, flat_ref):
    tile = pl.program_id(0)
    rows = out_ref.shape[0]
    width = out_ref.shape[1]
    bins = out_ref.shape[2] // 2
    pair = 2 * GROUP
    groups = bins // GROUP
    depth = n * pair
    f32 = jnp.float32

    @pl.when(tile == 0)
    def _():
        first = lax.axis_index("chan") * rows
        mine = first // width
        chosen = (
            lax.broadcasted_iota(jnp.int32, (rows, width), 1)
            == lax.broadcasted_iota(jnp.int32, (rows, width), 0) + lax.rem(first, width)
        )
        chosen = jnp.where(chosen, 1.0, 0.0).astype(jnp.bfloat16)
        lane = lax.broadcasted_iota(jnp.int32, (rows, depth), 1)
        imag_lane = lax.rem(lane, pair) >= GROUP
        lane8 = lax.broadcasted_iota(jnp.int32, (GROUP, depth), 1)
        keep = jnp.where(
            lax.rem(lane8, GROUP) == lax.broadcasted_iota(jnp.int32, (GROUP, depth), 0), 1.0, 0.0
        )

        @pl.loop(0, groups)
        def _(g):
            at = pl.multiple_of(g * pair, pair)
            right = all_ref[:, mine, pl.ds(at, pair), :].reshape(depth, width)
            own = lax.dot_general(
                chosen, right, (((1,), (1,)), ((), ())), preferred_element_type=f32
            )
            turned = jnp.where(
                imag_lane, -pltpu.roll(own, GROUP, 1), pltpu.roll(own, depth - GROUP, 1)
            )
            for part, values in enumerate((own, turned)):
                spread = jnp.concatenate(
                    [jnp.broadcast_to(values[i : i + 1], (GROUP, depth)) * keep for i in range(rows)], 0
                )
                left_ref[g, pl.ds(part * rows * GROUP, rows * GROUP), :] = spread.astype(jnp.bfloat16)

    @pl.loop(0, groups)
    def _(g):
        at = pl.multiple_of(g * pair, pair)
        right = all_ref[:, tile, pl.ds(at, pair), :].reshape(depth, width)
        value = jnp.dot(left_ref[g], right, preferred_element_type=f32) * scale
        flat_ref[:, pl.ds(pl.multiple_of(g * GROUP, GROUP), GROUP), :] = value.reshape(
            2 * rows, GROUP, width
        )

    eye = (
        lax.broadcasted_iota(jnp.int32, (width, width), 0)
        == lax.broadcasted_iota(jnp.int32, (width, width), 1)
    )
    eye = jnp.where(eye, 1.0, 0.0).astype(jnp.bfloat16)

    @pl.loop(0, rows)
    def _(i):
        both = jnp.concatenate([flat_ref[i], flat_ref[rows + i]], 0).astype(jnp.bfloat16)
        out_ref[i] = lax.dot_general(
            eye, both, (((1,), (1,)), ((), ())), preferred_element_type=f32
        ).astype(jnp.bfloat16)


def per_device(n, raw_field, bin_list):
    raw_rows, channels = raw_field.shape
    bins = bin_list.shape[0]
    half_len = raw_rows // 4
    width = 256
    chunks = channels // width
    block = 128
    reach = n // 4
    bf16, f32 = jnp.bfloat16, jnp.float32
    band = jnp.asarray(band_matrix(block), bf16)
    dma = pltpu.SemaphoreType.DMA
    any_space = pl.BlockSpec(memory_space=pl.ANY)
    vmem = pl.BlockSpec(memory_space=pltpu.VMEM)
    gathered = pl.pallas_call(
        functools.partial(gather_kernel, n),
        out_shape=jax.ShapeDtypeStruct((n, chunks, 2 * bins, width), bf16),
        in_specs=[any_space, vmem, vmem],
        out_specs=any_space,
        scratch_shapes=[
            pltpu.VMEM((chunks, TAPS + raw_rows, width), bf16),
            pltpu.VMEM((2, 2 * bins, half_len), bf16),
            pltpu.VMEM((half_len, width), bf16),
            pltpu.VMEM((chunks, 2 * bins, width), f32),
            pltpu.VMEM((chunks, 2 * bins, width), bf16),
            pltpu.VMEM((chunks, 2 * bins, width), bf16),
            pltpu.VMEM((chunks, 2 * bins, width), bf16),
        ]
        + [dma((chunks,))] * 8
        + [dma((2, chunks, reach))] * 4,
        compiler_params=pltpu.CompilerParams(
            collective_id=0, has_side_effects=True, vmem_limit_bytes=40 * 2**20
        ),
        name="gather_spectra",
    )(raw_field, bin_list.reshape(1, bins), band)

    positions = np.arange(2 * half_len)
    power = float(np.sum(np.sin(np.pi * positions / (2 * half_len)) ** 4))
    rows = channels // n
    return pl.pallas_call(
        functools.partial(cross_kernel, n, 1.0 / ((n - 1) * power)),
        grid=(chunks,),
        out_shape=jax.ShapeDtypeStruct((rows, channels, 2 * bins), bf16),
        in_specs=[
            pl.BlockSpec(
                (n, chunks, 2 * bins, width), lambda j: (0, 0, 0, 0), pipeline_mode=pl.Buffered(1)
            )
        ],
        out_specs=pl.BlockSpec((rows, width, 2 * bins), lambda j: (0, j, 0)),
        scratch_shapes=[
            pltpu.VMEM((bins // GROUP, 2 * rows * GROUP, n * 2 * GROUP), bf16),
            pltpu.VMEM((2 * rows, bins, width), f32),
        ],
        compiler_params=pltpu.CompilerParams(vmem_limit_bytes=56 * 2**20),
        name="cross_products",
    )(gathered)


def solution(mesh):
    return jax.shard_map(
        functools.partial(per_device, mesh.shape["chan"]),
        mesh=mesh,
        in_specs=(P("chan", "sections"), P()),
        out_specs=P(("sections", "chan"), None, None),
        check_vma=False,
    )
```

time: 646 us -> 72.8 us (0.11); the launches traced: 635 us -> 72.6 us
  local copies, waits for them, and re-layouts: 231 us -> 5.69 us
  matrix products: 198 us -> 0 us
  waiting for transfers between devices: 140 us -> 0 us
  Pallas kernels: 0 us -> 66.9 us
  other arithmetic: 46.5 us -> 0 us
  starting transfers between devices: 17.3 us -> 0 us
    dot_general x74 -> x0, matrix products: 198 us -> none  [the longest x64 153 us: inner(): jnp.einsum('sif,sjf->ijf', first_op, second_op, preferred_element_type=jn...]
    ppermute x17 -> x0, waiting for transfers between devices: 132 us -> none  [the longest x15 127 us: passed_along(): lax.ppermute(x, axis, [(i, (i + by) % length) for i in range(length)])]
    slice x28 -> x0, local copies, waits for them, and re-layouts: 69.2 us -> none  [the longest x10 66.8 us: decimate(): window_rows = grouped[block:block + out_rows]]
    pallas_call x0 -> x2, Pallas kernels: none -> 66.9 us  [the longest x1 36 us: per_device(): pl.pallas_call(functools.partial(gather_kernel, n), out_shape=jax.ShapeDt...]
    add x16 -> x0, local copies, waits for them, and re-layouts: 55.3 us -> none  [cross_parts(): real_part = inner(left_re, right_re) + inner(left_im, right_im)]
    sub x16 -> x0, local copies, waits for them, and re-layouts: 42.5 us -> none  [cross_parts(): imag_part = inner(left_im, right_re) - inner(left_re, right_im)]
    while x75 -> x0, local copies, waits for them, and re-layouts: 36.2 us -> none
    dynamic_update_slice x16 -> x0, other arithmetic: 29 us -> none  [place_block(): lax.dynamic_update_slice(output, product, (zero_index, source * block_col...]
  transfers between devices with their start and end apart: 18 -> 0, of which waited for: 17 -> 0; matrix products, arithmetic and copies ran while one was open for 3% -> 0% of each run, Pallas kernels for 0% -> 0%
where the time goes in v1:
time: 72.8 us; the launch traced here: 72.6 us
  Pallas kernels  66.9 us (92%)
  local copies, waits for them, and re-layouts  5.69 us (8%)
    pallas_call x1, Pallas kernels, per_device(): pl.pallas_call(functools.partial(gather_kernel, n), out_shape=jax.ShapeDt...  36 us
    pallas_call x1, Pallas kernels, per_device(): pl.pallas_call(functools.partial(cross_kernel, n, 1.0 / ((n - 1) * power)...  30.9 us
    unnamed x8, local copies, waits for them, and re-layouts  5.69 us

profile of v1, /device:TPU:0, one launch (start us, length us, event | category | flops | bytes accessed | tf_op | source)
XLA Modules:
  0.0 72.6 jit_solution(7561651420236995941)
XLA Ops:
  0.0 0.0 copy-start.1
  0.0 2.2 %copy-done.1 = bf16[4096,512]{1,0:T(8,128)(2,1)S(1)} copy-done((bf16[4096,512]{1,0:T(8,128)(2,1)S(1)}, bf16[4096,512]{1,0:T(8,128)(2,1)}, u32[]{:S(2)}) %copy-start.1) | copy-done | bytes 4194328
  2.2 0.0 copy-start.2
  2.2 0.9 %copy-done.2 = bf16[128,544]{1,0:T(8,128)(2,1)S(1)} copy-done((bf16[128,544]{1,0:T(8,128)(2,1)S(1)}, bf16[128,544]{1,0:T(8,128)(2,1)}, u32[]{:S(2)}) %copy-start.2) | copy-done | bytes 139288
  3.1 0.0 copy-start.3
  3.1 0.7 copy-done.3
  3.8 36.0 %gather_spectra.1.all_ref = bf16[16,2,256,256]{3,2,1,0:T(8,128)(2,1)S(1)} custom-call(bf16[4096,512]{1,0:T(8,128)(2,1)S(1)} %copy-done.1, s32[1,128]{1,0:T(1,128)S(1)} %bitcast.1, bf16[128,544]{1,0:T(8,128)(2,1)S(1)} %copy-done.2), custom_call_target="tpu_custom_call" | custom-call | tf_op jit(solution)/shard_map/gather_spectra/pallas_call | solution.py:317
  39.8 0.0 copy-start
  39.8 1.9 %copy-done = bf16[16,2,256,256]{3,2,1,0:T(8,128)(2,1)} copy-done((bf16[16,2,256,256]{3,2,1,0:T(8,128)(2,1)}, bf16[16,2,256,256]{3,2,1,0:T(8,128)(2,1)S(1)}, u32[]{:S(2)}) %copy-start) | copy-done | bytes 4194328
  41.7 30.9 %cross_products.1 = bf16[32,512,256]{2,1,0:T(8,128)(2,1)} custom-call(bf16[16,2,256,256]{3,2,1,0:T(8,128)(2,1)} %copy-done), custom_call_target="tpu_custom_call" | custom-call | tf_op jit(solution)/shard_map/cross_products/pallas_call | solution.py:342
Async XLA Ops:
  0.0 2.2 %copy-start.1 = (bf16[4096,512]{1,0:T(8,128)(2,1)S(1)}, bf16[4096,512]{1,0:T(8,128)(2,1)}, u32[]{:S(2)}) copy-start(bf16[4096,512]{1,0:T(8,128)(2,1)} %raw_ref.1) | copy-start | bytes 12582916
  2.2 0.9 %copy-start.2 = (bf16[128,544]{1,0:T(8,128)(2,1)S(1)}, bf16[128,544]{1,0:T(8,128)(2,1)}, u32[]{:S(2)}) copy-start(bf16[128,544]{1,0:T(8,128)(2,1)} %constant.2.clone.band_ref) | copy-start | bytes 417796
  3.1 0.7 copy-start.3
  39.8 1.9 %copy-start = (bf16[16,2,256,256]{3,2,1,0:T(8,128)(2,1)}, bf16[16,2,256,256]{3,2,1,0:T(8,128)(2,1)S(1)}, u32[]{:S(2)}) copy-start(bf16[16,2,256,256]{3,2,1,0:T(8,128)(2,1)S(1)} %gather_spectra.1.all_ref) | copy-start | bytes 12582916

commit v2 on v1

--- a/solution.py
+++ b/solution.py
@@ -25,13 +25,24 @@
     return np.array([value / total for value in shaped], np.float64)
 
 
-def band_matrix(out_rows):
-    h = lowpass_taps()
-    n = np.arange(out_rows)[:, None]
-    m = np.arange(TAPS + 4 * out_rows)[None, :] - TAPS
-    k = 4 * n - m
-    inside = (k >= 0) & (k < TAPS)
-    return np.where(inside, h[np.clip(k, 0, TAPS - 1)], 0.0)
+def write_band(band_ref):
+    rows, span = band_ref.shape
+    taps = lowpass_taps()
+    pieces = []
+    for top in range(0, rows, 8):
+        tiles = []
+        for left in range(0, span, 128):
+            wide = min(128, span - left)
+            value = jnp.zeros((8, wide), jnp.float32)
+            if left <= 4 * top + 60 and 4 * top + 1 < left + wide:
+                row = lax.broadcasted_iota(jnp.int32, (8, wide), 0) + top
+                column = lax.broadcasted_iota(jnp.int32, (8, wide), 1) + left
+                offset = 4 * row + TAPS - column
+                for k in range(TAPS):
+                    value = jnp.where(offset == k, float(taps[k]), value)
+            tiles.append(value)
+        pieces.append(jnp.concatenate(tiles, 1))
+    band_ref[...] = jnp.concatenate(pieces, 0).astype(band_ref.dtype)
 
 
 def write_table(bins_ref, table_ref, half_len):
@@ -68,9 +79,9 @@
 
 
 def gather_kernel(
-    n, raw_ref, bins_ref, band_ref, all_ref,
-    raw_buf, table_ref, dec_ref, lead_ref, trail_out, trail_in, own_ref,
-    raw_sem, halo_send, halo_recv, trail_send, trail_recv,
+    n, raw_ref, bins_hbm, all_ref,
+    raw_buf, bins_ref, band_ref, table_ref, dec_ref, lead_ref, trail_out, trail_in, own_ref,
+    bins_sem, raw_sem, halo_send, halo_recv, trail_send, trail_recv,
     own_sem, own_sib_send, own_sib_recv, ring_send, ring_recv, sib_send, sib_recv,
 ):
     chunks, _, width = raw_buf.shape
@@ -106,12 +117,15 @@
             device_id={"chan": target}, device_id_type=MESH,
         )
 
+    bins_copy = pltpu.make_async_copy(bins_hbm, bins_ref, bins_sem)
+    bins_copy.start()
     for c in range(chunks):
         raw_copy(c).start()
     barrier = pltpu.get_barrier_semaphore()
     partners = neighbours + (sibling, after, before)
     for partner in partners:
         pl.semaphore_signal(barrier, inc=1, device_id={"chan": partner}, device_id_type=MESH)
+    write_band(band_ref)
     pl.semaphore_wait(barrier, len(partners))
 
     def halo_copy(c):
@@ -138,6 +152,7 @@
     def _():
         trail_in[...] = jnp.zeros(trail_in.shape, trail_in.dtype)
 
+    bins_copy.wait()
     write_table(bins_ref, table_ref, half_len)
 
     for c in range(chunks):
@@ -236,69 +251,64 @@
                 sib_copy(way, c, t - 1, owner(way, t, 1 - core)).wait_recv()
 
 
-def cross_kernel(n, scale, all_ref, out_ref, left_ref, flat_ref):
-    tile = pl.program_id(0)
+def cross_kernel(n, scale, all_ref, out_ref, left_ref, flat_ref, stage_ref, out_sem):
     rows = out_ref.shape[0]
-    width = out_ref.shape[1]
+    chunks, width = all_ref.shape[1], all_ref.shape[3]
     bins = out_ref.shape[2] // 2
     pair = 2 * GROUP
     groups = bins // GROUP
     depth = n * pair
     f32 = jnp.float32
 
-    @pl.when(tile == 0)
-    def _():
-        first = lax.axis_index("chan") * rows
-        mine = first // width
-        chosen = (
-            lax.broadcasted_iota(jnp.int32, (rows, width), 1)
-            == lax.broadcasted_iota(jnp.int32, (rows, width), 0) + lax.rem(first, width)
-        )
-        chosen = jnp.where(chosen, 1.0, 0.0).astype(jnp.bfloat16)
-        lane = lax.broadcasted_iota(jnp.int32, (rows, depth), 1)
-        imag_lane = lax.rem(lane, pair) >= GROUP
-        lane8 = lax.broadcasted_iota(jnp.int32, (GROUP, depth), 1)
-        keep = jnp.where(
-            lax.rem(lane8, GROUP) == lax.broadcasted_iota(jnp.int32, (GROUP, depth), 0), 1.0, 0.0
-        )
-
-        @pl.loop(0, groups)
-        def _(g):
-            at = pl.multiple_of(g * pair, pair)
-            right = all_ref[:, mine, pl.ds(at, pair), :].reshape(depth, width)
-            own = lax.dot_general(
-                chosen, right, (((1,), (1,)), ((), ())), preferred_element_type=f32
-            )
-            turned = jnp.where(
-                imag_lane, -pltpu.roll(own, GROUP, 1), pltpu.roll(own, depth - GROUP, 1)
-            )
-            for part, values in enumerate((own, turned)):
-                spread = jnp.concatenate(
-                    [jnp.broadcast_to(values[i : i + 1], (GROUP, depth)) * keep for i in range(rows)], 0
-                )
-                left_ref[g, pl.ds(part * rows * GROUP, rows * GROUP), :] = spread.astype(jnp.bfloat16)
-
-    @pl.loop(0, groups)
+    first = lax.axis_index("chan") * rows
+    mine = first // width
+    chosen = (
+        lax.broadcasted_iota(jnp.int32, (rows, width), 1)
+        == lax.broadcasted_iota(jnp.int32, (rows, width), 0) + lax.rem(first, width)
+    )
+    chosen = jnp.where(chosen, 1.0, 0.0).astype(jnp.bfloat16)
+    imag_lane = lax.rem(lax.broadcasted_iota(jnp.int32, (rows, depth), 1), pair) >= GROUP
+    lane8 = lax.broadcasted_iota(jnp.int32, (GROUP, depth), 1)
+    keep = lax.rem(lane8, GROUP) == lax.broadcasted_iota(jnp.int32, (GROUP, depth), 0)
+    keep = jnp.where(keep, 1.0, 0.0)
+
+    @pl.loop(0, groups, unroll=4)
     def _(g):
         at = pl.multiple_of(g * pair, pair)
-        right = all_ref[:, tile, pl.ds(at, pair), :].reshape(depth, width)
+        own = lax.dot_general(
+            chosen,
+            all_ref[:, mine, pl.ds(at, pair), :].reshape(depth, width),
+            (((1,), (1,)), ((), ())),
+            preferred_element_type=f32,
+        )
+        turned = jnp.where(
+            imag_lane, -pltpu.roll(own, GROUP, 1), pltpu.roll(own, depth - GROUP, 1)
+        )
+        for part, values in enumerate((own, turned)):
+            spread = jnp.concatenate(
+                [jnp.broadcast_to(values[i : i + 1], (GROUP, depth)) * keep for i in range(rows)], 0
+            )
+            left_ref[g, pl.ds(part * rows * GROUP, rows * GROUP), :] = spread.astype(jnp.bfloat16)
+        right = jnp.concatenate(
+            [all_ref[:, c, pl.ds(at, pair), :].reshape(depth, width) for c in range(chunks)], 1
+        )
         value = jnp.dot(left_ref[g], right, preferred_element_type=f32) * scale
         flat_ref[:, pl.ds(pl.multiple_of(g * GROUP, GROUP), GROUP), :] = value.reshape(
-            2 * rows, GROUP, width
-        )
-
-    eye = (
-        lax.broadcasted_iota(jnp.int32, (width, width), 0)
-        == lax.broadcasted_iota(jnp.int32, (width, width), 1)
-    )
-    eye = jnp.where(eye, 1.0, 0.0).astype(jnp.bfloat16)
+            2 * rows, GROUP, chunks * width
+        )
+
+    def out_copy(i):
+        return pltpu.make_async_copy(stage_ref.at[i], out_ref.at[i], out_sem.at[i])
+
+    @pl.loop(0, rows, unroll=4)
+    def _(i):
+        both = jnp.concatenate([flat_ref[i], flat_ref[rows + i]], 0).astype(jnp.bfloat16)
+        stage_ref[i] = both.T
+        out_copy(i).start()
 
     @pl.loop(0, rows)
     def _(i):
-        both = jnp.concatenate([flat_ref[i], flat_ref[rows + i]], 0).astype(jnp.bfloat16)
-        out_ref[i] = lax.dot_general(
-            eye, both, (((1,), (1,)), ((), ())), preferred_element_type=f32
-        ).astype(jnp.bfloat16)
+        out_copy(i).wait()
 
 
 def per_device(n, raw_field, bin_list):
@@ -310,17 +320,18 @@
     block = 128
     reach = n // 4
     bf16, f32 = jnp.bfloat16, jnp.float32
-    band = jnp.asarray(band_matrix(block), bf16)
     dma = pltpu.SemaphoreType.DMA
-    any_space = pl.BlockSpec(memory_space=pl.ANY)
+    hbm = pl.BlockSpec(memory_space=pltpu.HBM)
     vmem = pl.BlockSpec(memory_space=pltpu.VMEM)
     gathered = pl.pallas_call(
         functools.partial(gather_kernel, n),
         out_shape=jax.ShapeDtypeStruct((n, chunks, 2 * bins, width), bf16),
-        in_specs=[any_space, vmem, vmem],
-        out_specs=any_space,
+        in_specs=[hbm, hbm],
+        out_specs=vmem,
         scratch_shapes=[
             pltpu.VMEM((chunks, TAPS + raw_rows, width), bf16),
+            pltpu.VMEM((1, bins), jnp.int32),
+            pltpu.VMEM((block, TAPS + 4 * block), bf16),
             pltpu.VMEM((2, 2 * bins, half_len), bf16),
             pltpu.VMEM((half_len, width), bf16),
             pltpu.VMEM((chunks, 2 * bins, width), f32),
@@ -328,32 +339,32 @@
             pltpu.VMEM((chunks, 2 * bins, width), bf16),
             pltpu.VMEM((chunks, 2 * bins, width), bf16),
         ]
+        + [dma]
         + [dma((chunks,))] * 8
         + [dma((2, chunks, reach))] * 4,
         compiler_params=pltpu.CompilerParams(
-            collective_id=0, has_side_effects=True, vmem_limit_bytes=40 * 2**20
+            collective_id=0,
+            has_side_effects=True,
+            vmem_limit_bytes=50 * 2**20 - n * channels * 2 * bins * 2,
         ),
         name="gather_spectra",
-    )(raw_field, bin_list.reshape(1, bins), band)
+    )(raw_field, bin_list.reshape(1, bins))
 
     positions = np.arange(2 * half_len)
     power = float(np.sum(np.sin(np.pi * positions / (2 * half_len)) ** 4))
     rows = channels // n
     return pl.pallas_call(
         functools.partial(cross_kernel, n, 1.0 / ((n - 1) * power)),
-        grid=(chunks,),
         out_shape=jax.ShapeDtypeStruct((rows, channels, 2 * bins), bf16),
-        in_specs=[
-            pl.BlockSpec(
-                (n, chunks, 2 * bins, width), lambda j: (0, 0, 0, 0), pipeline_mode=pl.Buffered(1)
-            )
-        ],
-        out_specs=pl.BlockSpec((rows, width, 2 * bins), lambda j: (0, j, 0)),
+        in_specs=[vmem],
+        out_specs=hbm,
         scratch_shapes=[
             pltpu.VMEM((bins // GROUP, 2 * rows * GROUP, n * 2 * GROUP), bf16),
-            pltpu.VMEM((2 * rows, bins, width), f32),
+            pltpu.VMEM((2 * rows, bins, channels), f32),
+            pltpu.VMEM((rows, channels, 2 * bins), bf16),
+            dma((rows,)),
         ],
-        compiler_params=pltpu.CompilerParams(vmem_limit_bytes=56 * 2**20),
+        compiler_params=pltpu.CompilerParams(vmem_limit_bytes=40 * 2**20),
         name="cross_products",
     )(gathered)
 

time: 72.8 us -> 45.7 us (0.63)
  Pallas kernels: 66.9 us -> 44.9 us
  local copies, waits for them, and re-layouts: 5.69 us -> 0.65 us
    pallas_call x1, Pallas kernels: 30.9 us -> 9.04 us  [per_device(): pl.pallas_call(functools.partial(cross_kernel, n, 1.0 / ((n - 1) * power)...]
    unnamed x8 -> x2, local copies, waits for them, and re-layouts: 5.69 us -> 0.65 us
where the time goes in v2:
time: 45.7 us; the launch traced here: 45.6 us
  Pallas kernels  44.9 us (98%)
  local copies, waits for them, and re-layouts  0.65 us (1%)
    pallas_call x1, Pallas kernels, per_device(): pl.pallas_call(functools.partial(gather_kernel, n), out_shape=jax.ShapeDt...  35.9 us
    pallas_call x1, Pallas kernels, per_device(): pl.pallas_call(functools.partial(cross_kernel, n, 1.0 / ((n - 1) * power)...  9.04 us

profile of v2, /device:TPU:0, one launch (start us, length us, event | category | flops | bytes accessed | tf_op | source)
XLA Modules:
  0.0 45.6 jit_solution(16782594455847490202)
XLA Ops:
  0.0 0.0 copy-start
  0.0 0.7 %copy-done = s32[128]{0:T(128)S(1)} copy-done((s32[128]{0:T(128)S(1)}, s32[128]{0:T(128)}, u32[]{:S(2)}) %copy-start) | copy-done | bytes 536
  0.7 35.9 %gather_spectra.1.all_ref = bf16[16,2,256,256]{3,2,1,0:T(8,128)(2,1)S(1)} custom-call(bf16[4096,512]{1,0:T(8,128)(2,1)} %raw_ref.1, s32[1,128]{1,0:T(1,128)S(1)} %bitcast.1), custom_call_target="tpu_custom_call" | custom-call | tf_op jit(solution)/shard_map/gather_spectra/pallas_call | solution.py:326
  36.6 9.0 %cross_products.1 = bf16[32,512,256]{2,1,0:T(8,128)(2,1)} custom-call(bf16[16,2,256,256]{3,2,1,0:T(8,128)(2,1)S(1)} %gather_spectra.1.all_ref), custom_call_target="tpu_custom_call" | custom-call | tf_op jit(solution)/shard_map/cross_products/pallas_call | solution.py:356
Async XLA Ops:
  0.0 0.7 %copy-start = (s32[128]{0:T(128)S(1)}, s32[128]{0:T(128)}, u32[]{:S(2)}) copy-start(s32[128]{0:T(128)} %param.3) | copy-start | bytes 1540

commit v3 on v2

--- a/solution.py
+++ b/solution.py
@@ -272,7 +272,7 @@
     keep = lax.rem(lane8, GROUP) == lax.broadcasted_iota(jnp.int32, (GROUP, depth), 0)
     keep = jnp.where(keep, 1.0, 0.0)
 
-    @pl.loop(0, groups, unroll=4)
+    @pl.loop(0, groups, unroll=16)
     def _(g):
         at = pl.multiple_of(g * pair, pair)
         own = lax.dot_general(
@@ -300,7 +300,7 @@
     def out_copy(i):
         return pltpu.make_async_copy(stage_ref.at[i], out_ref.at[i], out_sem.at[i])
 
-    @pl.loop(0, rows, unroll=4)
+    @pl.loop(0, rows, unroll=min(rows, 16))
     def _(i):
         both = jnp.concatenate([flat_ref[i], flat_ref[rows + i]], 0).astype(jnp.bfloat16)
         stage_ref[i] = both.T

time: 45.7 us -> 45.1 us (0.987)
  Pallas kernels: 44.9 us -> 44.2 us
    pallas_call x1, Pallas kernels: 9.04 us -> 8.35 us  [per_device(): pl.pallas_call(functools.partial(cross_kernel, n, 1.0 / ((n - 1) * power)...]
where the time goes in v3:
time: 45.1 us; the launch traced here: 44.9 us
  Pallas kernels  44.2 us (98%)
  local copies, waits for them, and re-layouts  0.65 us (1%)
    pallas_call x1, Pallas kernels, per_device(): pl.pallas_call(functools.partial(gather_kernel, n), out_shape=jax.ShapeDt...  35.9 us
    pallas_call x1, Pallas kernels, per_device(): pl.pallas_call(functools.partial(cross_kernel, n, 1.0 / ((n - 1) * power)...  8.35 us

profile of v3, /device:TPU:0, one launch (start us, length us, event | category | flops | bytes accessed | tf_op | source)
XLA Modules:
  0.0 44.9 jit_solution(14967792713932713174)
XLA Ops:
  0.0 0.0 copy-start
  0.0 0.7 %copy-done = s32[128]{0:T(128)S(1)} copy-done((s32[128]{0:T(128)S(1)}, s32[128]{0:T(128)}, u32[]{:S(2)}) %copy-start) | copy-done | bytes 536
  0.7 35.9 %gather_spectra.1.all_ref = bf16[16,2,256,256]{3,2,1,0:T(8,128)(2,1)S(1)} custom-call(bf16[4096,512]{1,0:T(8,128)(2,1)} %raw_ref.1, s32[1,128]{1,0:T(1,128)S(1)} %bitcast.1), custom_call_target="tpu_custom_call" | custom-call | tf_op jit(solution)/shard_map/gather_spectra/pallas_call | solution.py:326
  36.6 8.4 %cross_products.1 = bf16[32,512,256]{2,1,0:T(8,128)(2,1)} custom-call(bf16[16,2,256,256]{3,2,1,0:T(8,128)(2,1)S(1)} %gather_spectra.1.all_ref), custom_call_target="tpu_custom_call" | custom-call | tf_op jit(solution)/shard_map/cross_products/pallas_call | solution.py:356
Async XLA Ops:
  0.0 0.7 %copy-start = (s32[128]{0:T(128)S(1)}, s32[128]{0:T(128)}, u32[]{:S(2)}) copy-start(s32[128]{0:T(128)} %param.3) | copy-start | bytes 1540
